TPU v7x, 256 devices: a whole 4x4x8 slice. The times are simulated.
256 devices in a mesh: group: 8 (over z), dev: 32 (over x, y, core).
Axes of the slice: x: 4, y: 4, z: 8, core: 2. Of those that a mesh axis runs over, the one named last changes fastest.
Arguments:
- corpus_rows: bfloat16 [524288, 1024], P(('group', 'dev')), may hold values from -16 to 16
- list_ids: int32 [524288], P(('group', 'dev')), may hold values from 0 to 65535, as said below
- source_ids: int32 [524288], P(('group', 'dev')), may hold values from 0 to 999999
- list_slot: int32 [65536], replicated, may hold values from 0 to 65535, as said below
- centroids: bfloat16 [65536, 1024], P('dev'), may hold values from -13 to 13
- start_basis: float32 [1024, 256], replicated, may hold values from -6 to 6
Outputs:
- row_codes: bfloat16 [1310720, 256], P(('group', 'dev'))
- row_sources: int32 [1310720], P(('group', 'dev'))
- list_counts: int32 [65536], P('dev')
Inputs may be any that keep to these rules, and one draw needn't show every extreme that they name: A permutation; the centroid of list l is row list_slot[l] of centroids. For each device, at most 160 of its rows have an owner list_slot[list_ids] // 2048 equal to any one index o; in every draw one owner of each group takes exactly 160 rows from every device of that group.
All inputs are finite; a program needn't handle non-finite values.
Results may differ from a plain program's by a relative error of at most 0.001.
Values may be sent and summed in bfloat16 or wider, within the bound.
A program may use at most 128 MiB of HBM per device.

v0:
```python
import functools
import jax
import jax.numpy as jnp
from jax import lax
from jax.experimental import pallas as pl
from jax.experimental.pallas import tpu as pltpu
from jax.sharding import PartitionSpec as P

CAP = 160
MESH = pl.DeviceIdType.MESH
NT = (((1,), (1,)), ((), ()))
TN = (((0,), (0,)), ((), ()))
HALF, MID, LOW = 1152, 288, 72
PAIRS = ((0, 0), (1, 0), (1, 1), (2, 0), (2, 1), (2, 2), (3, 0), (3, 1), (3, 2), (3, 3))


def block_starts():
    starts = {}
    for i, j in PAIRS:
        for a in range(2):
            for b in range(2):
                if 2 * j + b <= 2 * i + a:
                    starts[(2 * i + a, 2 * j + b)] = len(starts) * 128
    return starts


STARTS = block_starts()


def vmem():
    return pl.BlockSpec(memory_space=pltpu.VMEM)


def smem():
    return pl.BlockSpec(memory_space=pltpu.SMEM)


def limits():
    return pltpu.CompilerParams(vmem_limit_bytes=48 * 2**20)


def halves(v):
    top = v.astype(jnp.bfloat16)
    return top, (v - top.astype(jnp.float32)).astype(jnp.bfloat16)


def dot(a, b, dims=(((1,), (0,)), ((), ()))):
    return lax.dot_general(a, b, dims, preferred_element_type=jnp.float32)


def packed_rows(cap):
    return cap + cap // 2 + 8


def narrow(flag):
    return flag.astype(jnp.float32).astype(jnp.bfloat16)


def place_rows(ids, source, table, owners, lists_dev, cap):
    count = ids.shape[1]
    sub = lax.broadcasted_iota(jnp.int32, (table.shape[0], count), 0)
    row_hit = narrow(sub == ids // 128)
    high = dot((table // 256).astype(jnp.float32).astype(jnp.bfloat16), row_hit, TN)
    low = dot((table % 256).astype(jnp.float32).astype(jnp.bfloat16), row_hit, TN)
    lane = lax.broadcasted_iota(jnp.int32, (128, count), 0)
    slot = jnp.sum(jnp.where(lane == ids % 128, high * 256.0 + low, 0.0), axis=0, keepdims=True).astype(jnp.int32)
    owner = slot // lists_dev
    local = slot % lists_dev
    owner_one = narrow(lax.broadcasted_iota(jnp.int32, (owners, count), 0) == owner)
    width = 256
    square = (width, width)
    before = narrow(lax.broadcasted_iota(jnp.int32, square, 0) < lax.broadcasted_iota(jnp.int32, square, 1))
    seen = jnp.zeros((owners, 1), jnp.float32)
    ranks = []
    for k in range(count // width):
        part = owner_one[:, k * width:(k + 1) * width]
        prior = dot(part, before) + seen
        part = part.astype(jnp.float32)
        ranks.append(jnp.sum(prior * part, axis=0, keepdims=True))
        seen = seen + jnp.sum(part, axis=1, keepdims=True)
    rank = jnp.concatenate(ranks, axis=1).astype(jnp.int32)
    rank_hit = lax.broadcasted_iota(jnp.int32, (256, count), 0) == rank

    def collect(value):
        picked = jnp.where(rank_hit, value.astype(jnp.float32), 0.0).astype(jnp.bfloat16)
        return dot(owner_one, picked, NT)

    filled = collect(jnp.ones((1, count), jnp.int32)) > 0.5
    local_at = collect(local // 256) * 256.0 + collect(local % 256)
    source_at = collect(source // 16384) * 16384.0 + collect((source // 128) % 128) * 128.0 + collect(source % 128)
    ids_at = jnp.where(filled, local_at, -1.0).astype(jnp.int32)
    sources_at = jnp.where(filled, source_at, -1.0).astype(jnp.int32)
    pos = jnp.concatenate([owner * cap + rank, owner * packed_rows(cap) + rank], axis=0)
    return pos, ids_at, sources_at


def front_kernel(lists_dev, cap, x_hbm, list_hbm, source_hbm, table_hbm, tri_ref, pos_ref, got_ref, count_ref,
                 x_ref, list_ref, source_ref, table_ref, load_s, dest, part, core_buf, first_buf, sum_buf, second_buf, mid_sum, tile_buf, tally, tally_buf,
                 core_s, core_r, first_s, first_r, second_s, second_r, tile_s, tile_r, top_s, top_r, odd_s, odd_r,
                 fan_s, fan_r, row_s, row_r, pair_s, pair_r, wide_s, wide_r, id_s, id_r, tally_s, tally_r):
    z = lax.axis_index("group")
    dev = lax.axis_index("dev")
    owners = 32
    x, y, c = dev // 8, (dev // 2) % 4, dev % 2

    def at(xx, yy):
        return (z, (xx * 4 + yy) * 2 + c)

    other = (z, dev + 1 - 2 * c)
    along_x = [at((x + d) % 4, y) for d in (1, 2, 3)]
    along_y = [at(x, (y + d) % 4) for d in (1, 2, 3)]
    along_z = [((z + d) % 8, dev) for d in range(1, 8)]
    barrier = pltpu.get_barrier_semaphore()
    for k in range(1, owners):
        pl.semaphore_signal(barrier, inc=1, device_id=(z, (dev + k) % owners), device_id_type=MESH)
    for peer in along_z:
        pl.semaphore_signal(barrier, inc=1, device_id=peer, device_id_type=MESH)

    loads = [
        pltpu.make_async_copy(list_hbm, list_ref, load_s.at[4]),
        pltpu.make_async_copy(source_hbm, source_ref, load_s.at[5]),
        pltpu.make_async_copy(table_hbm, table_ref, load_s.at[6]),
    ]
    for k in range(4):
        columns = pl.ds(k * 256, 256)
        loads.append(pltpu.make_async_copy(x_hbm.at[:, columns], x_ref.at[:, columns], load_s.at[k]))
    for load in loads[3:] + loads[:3]:
        load.start()
    sent = []

    def copy_to(src, dst, s, r, peer):
        return pltpu.make_async_remote_copy(src_ref=src, dst_ref=dst, send_sem=s, recv_sem=r, device_id=peer,
                                            device_id_type=MESH)

    def send(src, dst, s, r, peer):
        copy = copy_to(src, dst, s, r, peer)
        copy.start()
        sent.append(copy)
        return copy

    def span(start, size):
        return pl.ds(pl.multiple_of(start, 8), size)

    lefts = {}

    def moment(pairs):
        for i, j in pairs:
            if i not in lefts:
                loads[3 + i].wait()
                lefts[i] = x_ref[:, i * 256:(i + 1) * 256].T
            square = dot(lefts[i], x_ref[:, j * 256:(j + 1) * 256])
            for a in range(2):
                for b in range(2):
                    key = (2 * i + a, 2 * j + b)
                    if key in STARTS:
                        begin = STARTS[key]
                        part[begin:begin + 128, :] = square[a * 128:(a + 1) * 128, b * 128:(b + 1) * 128]

    base = [p * 2 * HALF + c * HALF for p in range(2)]
    firsts = [(x, along_x), (y, along_y)]
    seconds = [(y, along_y), (x, along_x)]
    core = [None, None]
    first = [{}, {}]

    def swap(p):
        core[p] = send(part.at[span(p * 2 * HALF + (1 - c) * HALF, HALF)], core_buf.at[p], core_s.at[p], core_r.at[p],
                       other)

    def down_first(p):
        core[p].wait_recv()
        core_buf[p] = core_buf[p] + part[span(base[p], HALF), :]
        f, peers = firsts[p]
        s = seconds[p][0]
        for k in range(4):
            for d in (1, 2, 3):
                begin = ((f + d) % 4) * MID + ((s + 1 + k) % 4) * LOW
                first[p][k, d] = send(core_buf.at[p, span(begin, LOW)], first_buf.at[p, d - 1, k],
                                      first_s.at[p, d - 1, k], first_r.at[p, d - 1, k], peers[d - 1])

    moment(PAIRS[:5])
    pl.semaphore_wait(barrier, 38)
    swap(0)
    moment(PAIRS[5:8])
    down_first(0)
    moment(PAIRS[8:])
    swap(1)
    down_first(1)
    for load in loads[:3]:
        load.wait()
    pos, ids_at, sources_at = place_rows(list_ref[...], source_ref[...], table_ref[...], owners, lists_dev, cap)
    pos_ref[...] = pos
    dest[:, 0, :] = ids_at[:, :128]
    dest[:, 1, :] = ids_at[:, 128:]
    dest[:, 2, :] = sources_at[:, :128]
    dest[:, 3, :] = sources_at[:, 128:]
    second = [{}, {}]
    for k in range(4):
        for p in range(2):
            f = firsts[p][0]
            s, peers = seconds[p]
            for d in (1, 2, 3):
                first[p][k, d].wait_recv()
            own = core_buf[p, span(f * MID + ((s + 1 + k) % 4) * LOW, LOW), :]
            sum_buf[p, k] = (own + first_buf[p, 0, k]) + (first_buf[p, 1, k] + first_buf[p, 2, k])
            if k < 3:
                second[p][k] = send(sum_buf.at[p, k], second_buf.at[p, k], second_s.at[p, k], second_r.at[p, k], peers[k])
    tile = [[], []]
    for p in range(2):
        for k in range(3):
            second[p][k].wait_recv()
        mid_sum[p] = (sum_buf[p, 3] + second_buf[p, 0]) + (second_buf[p, 1] + second_buf[p, 2])
        for d in range(1, 8):
            tile[p].append(send(mid_sum.at[p, span(((z + d) % 8) * 8, 16)], tile_buf.at[p, d - 1],
                                tile_s.at[p, d - 1], tile_r.at[p, d - 1], along_z[d - 1]))
    arrive = []
    for k in range(1, owners):
        peer = (dev + k) % owners
        arrive.append(send(dest.at[peer], got_ref.at[dev], id_s.at[k - 1], id_r.at[k - 1], (z, peer)))
    got_ref[dev] = dest[dev]
    def hand(begin, size, s, r, peer):
        return send(tri_ref.at[span(begin, size)], tri_ref.at[span(begin, size)], s, r, peer)

    top = [[], []]

    def odd(p, d):
        begin = base[p] + firsts[p][0] * MID + seconds[p][0] * LOW + 64
        return copy_to(tri_ref.at[span(begin, 8)], tri_ref.at[span(begin, 8)], odd_s.at[p, d - 1], odd_r.at[p],
                       along_z[d - 1])

    for p in range(2):
        for copy in tile[p]:
            copy.wait_recv()
        total = mid_sum[p, span(z * 8, 16), :]
        for d in range(7):
            total = total + tile_buf[p, d]
        begin = base[p] + firsts[p][0] * MID + seconds[p][0] * LOW
        tri_ref[span(begin + z * 8, 8), :] = total[:8]
        for d in range(1, 8):
            top[p].append(hand(begin + z * 8, 8, top_s.at[p, d - 1], top_r.at[p, d - 1], along_z[d - 1]))

        @pl.when(z == 7)
        def _():
            tri_ref[span(begin + 64, 8), :] = total[8:]
            for d in range(1, 8):
                odd(p, d).start()

    for copy in arrive:
        copy.wait_recv()
    ids = jnp.concatenate([got_ref[:, 0, :], got_ref[:, 1, :]], axis=0)
    ids = jnp.concatenate([ids[k:k + 1, :] for k in range(2 * owners)], axis=1)
    count = ids.shape[1]
    high = lax.broadcasted_iota(jnp.int32, (16, count), 0) == jnp.where(ids >= 0, ids // 128, -1)
    low = lax.broadcasted_iota(jnp.int32, (128, count), 0) == ids % 128
    tally[...] = dot(narrow(high), narrow(low), NT)
    tallies = [send(tally, tally_buf.at[d - 1], tally_s.at[d - 1], tally_r.at[d - 1], along_z[d - 1])
               for d in range(1, 8)]

    fan = [{}, {}]
    row = [{}, {}]
    pair = [[], []]

    def outward(p, k):
        f, peers = firsts[p]
        begin = base[p] + f * MID + ((seconds[p][0] - k + 4) % 4) * LOW
        for d in (1, 2, 3):
            row[p][k, d] = hand(begin, LOW, row_s.at[p, k, d - 1], row_r.at[p, k, d - 1], peers[d - 1])
        pair[p].append(hand(begin, LOW, pair_s.at[p, k], pair_r.at[p, k], other))

    for p in range(2):
        for copy in top[p]:
            copy.wait_recv()

        @pl.when(z != 7)
        def _():
            odd(p, 1).wait_recv()

        s, peers = seconds[p]
        begin = base[p] + firsts[p][0] * MID + s * LOW
        for d in (1, 2, 3):
            fan[p][d] = hand(begin, LOW, fan_s.at[p, d - 1], fan_r.at[p, d - 1], peers[d - 1])
        outward(p, 0)
    for d in (1, 2, 3):
        for p in range(2):
            fan[p][d].wait_recv()
            outward(p, d)
    total = tally[...]
    for d in range(7):
        tallies[d].wait_recv()
        total = total + tally_buf[d]
    count_ref[...] = total.astype(jnp.int32)
    wide = [[], []]
    for d in (1, 2, 3):
        for p in range(2):
            for k in range(4):
                row[p][k, d].wait_recv()
            begin = base[p] + ((firsts[p][0] - d + 4) % 4) * MID
            wide[p].append(hand(begin, MID, wide_s.at[p, d - 1], wide_r.at[p, d - 1], other))
    for p in range(2):
        for copy in pair[p] + wide[p]:
            copy.wait_recv()
    for copy in sent:
        copy.wait_send()

    @pl.when(z == 7)
    def _():
        for p in range(2):
            for d in range(1, 8):
                odd(p, d).wait_send()


def front(corpus_rows, list_ids, source_ids, list_slot, owners, lists_dev, cap):
    count = list_ids.shape[0]
    sem = pltpu.SemaphoreType.DMA
    f32 = jnp.float32
    return pl.pallas_call(
        functools.partial(front_kernel, lists_dev, cap),
        out_shape=(
            jax.ShapeDtypeStruct((4 * HALF, 128), f32),
            jax.ShapeDtypeStruct((2, count), jnp.int32),
            jax.ShapeDtypeStruct((owners, 4, 128), jnp.int32),
            jax.ShapeDtypeStruct((lists_dev // 128, 128), jnp.int32),
        ),
        in_specs=[pl.BlockSpec(memory_space=pl.ANY)] * 4,
        out_specs=(vmem(),) * 4,
        scratch_shapes=[
            pltpu.VMEM(corpus_rows.shape, jnp.bfloat16),
            pltpu.VMEM((1, count), jnp.int32),
            pltpu.VMEM((1, count), jnp.int32),
            pltpu.VMEM((list_slot.shape[0] // 128, 128), jnp.int32),
            sem((7,)),
            pltpu.VMEM((owners, 4, 128), jnp.int32),
            pltpu.VMEM((4 * HALF, 128), f32),
            pltpu.VMEM((2, HALF, 128), f32),
            pltpu.VMEM((2, 3, 4, LOW, 128), f32),
            pltpu.VMEM((2, 4, LOW, 128), f32),
            pltpu.VMEM((2, 3, LOW, 128), f32),
            pltpu.VMEM((2, LOW, 128), f32),
            pltpu.VMEM((2, 7, 16, 128), f32),
            pltpu.VMEM((16, 128), f32),
            pltpu.VMEM((7, 16, 128), f32),
            sem((2,)), sem((2,)), sem((2, 3, 4)), sem((2, 3, 4)), sem((2, 3)), sem((2, 3)), sem((2, 7)), sem((2, 7)),
            sem((2, 7)), sem((2, 7)), sem((2, 7)), sem((2,)), sem((2, 3)), sem((2, 3)), sem((2, 4, 3)), sem((2, 4, 3)),
            sem((2, 4)), sem((2, 4)), sem((2, 3)), sem((2, 3)), sem((31,)), sem((31,)), sem((7,)), sem((7,)),
        ],
        compiler_params=pltpu.CompilerParams(collective_id=0, has_side_effects=True, vmem_limit_bytes=60 * 2**20),
        cost_estimate=pl.CostEstimate(flops=10**10, bytes_accessed=10**8, transcendentals=0),
        name="front",
    )(corpus_rows, list_ids.reshape(1, count), source_ids.reshape(1, count), list_slot.reshape(-1, 128))


def step_of(exponent):
    return jnp.exp2((exponent - 23).astype(jnp.float32))


def project_rows(rows_ref, basis_ref, z_ref):
    count = rows_ref.shape[0]
    width = basis_ref.shape[1] // 2
    step = 1024
    for begin in range(0, count, step):
        both = dot(rows_ref[begin:begin + step, :], basis_ref[...])
        code = both[:, :width] + both[:, width:]
        z_ref[begin:begin + step, :] = code[:, :128]
        z_ref[count + begin:count + begin + step, :] = code[:, 128:]


def project_kernel(cap, tri_ref, start_ref, x_hbm, pos_ref, out_ref, basis_ref, gram_ref, x_ref, load_s, m_hi, m_lo,
                   z_ref, word_ref, tail_ref, sent_ref):
    load = pltpu.make_async_copy(x_hbm, x_ref, load_s)
    load.start()
    eye = lax.broadcasted_iota(jnp.int32, (128, 128), 0) == lax.broadcasted_iota(jnp.int32, (128, 128), 1)
    peak = jnp.zeros((128, 128), jnp.float32)
    for i in range(8):
        for j in range(i + 1):
            at = STARTS[(i, j)]
            block = tri_ref[at:at + 128, :]
            hi, lo = halves(block)
            m_hi[i * 128:(i + 1) * 128, j * 128:(j + 1) * 128] = hi
            m_lo[i * 128:(i + 1) * 128, j * 128:(j + 1) * 128] = lo
            if i != j:
                hi, lo = halves(block.T)
                m_hi[j * 128:(j + 1) * 128, i * 128:(i + 1) * 128] = hi
                m_lo[j * 128:(j + 1) * 128, i * 128:(i + 1) * 128] = lo
            else:
                peak = jnp.maximum(peak, jnp.where(eye, block, 0.0))
    scale = 1.0 / jnp.max(jnp.max(peak, axis=0, keepdims=True), axis=1, keepdims=True)
    width = start_ref.shape[1]

    def times_moment(v):
        hi, lo = halves(v * scale)
        both = dot(m_hi[...], jnp.concatenate([hi, lo], axis=1))
        return (both[:, :width] + both[:, width:]) + dot(m_lo[...], hi)

    product = times_moment(times_moment(start_ref[...]))
    product = product * lax.rsqrt(jnp.sum(product * product, axis=0, keepdims=True))
    hi, lo = halves(product)
    basis_ref[:, :width] = hi
    basis_ref[:, width:] = lo
    cross = dot(hi, basis_ref[...], TN)
    mixed = cross[:, width:]
    gram_ref[...] = cross[:, :width] + (mixed + mixed.T)
    load.wait()
    project_rows(x_ref, basis_ref, z_ref)
    count = x_ref.shape[0]

    peak = jnp.max(jnp.max(jnp.abs(z_ref[...]), axis=0, keepdims=True), axis=1, keepdims=True)
    lane = lax.broadcasted_iota(jnp.int32, (1, 128), 1)
    below = jnp.where(peak >= jnp.exp2((lane - 64).astype(jnp.float32)), 1.0, 0.0)
    exponent = jnp.sum(below, axis=1, keepdims=True).astype(jnp.int32) - 64
    unit = 1.0 / step_of(exponent)
    most = float(2**23 - 1)
    step = 256

    @pl.loop(0, count // step)
    def _(k):
        at = pl.multiple_of(k * step, step)

        def coded(begin):
            return jnp.clip(jnp.round(z_ref[pl.ds(begin, step), :] * unit), -most, most).astype(jnp.int32)

        low = coded(at)
        high = coded(pl.multiple_of(at + count, step))
        word_ref[pl.ds(at, step), :] = (low << 8) | (high & 255)
        upper = high >> 8
        tail_ref[pl.ds(at, step), :] = (upper << 16) | (pltpu.roll(upper, 64, 1) & 65535)

    @pl.loop(0, count // 16)
    def _(k):
        for u in range(16):
            row = k * 16 + u
            out_ref[pl.ds(pos_ref[1, row], 1), :] = word_ref[pl.ds(row, 1), :]
            sent_ref[pl.ds(pos_ref[0, row], 1), :] = tail_ref[pl.ds(row, 1), :]

    half = cap // 2
    left = lax.broadcasted_iota(jnp.int32, (half, 128), 1) < 64
    for owner in range(sent_ref.shape[0] // cap):
        begin = owner * packed_rows(cap) + cap
        first = sent_ref[owner * cap:owner * cap + half, :]
        second = sent_ref[owner * cap + half:(owner + 1) * cap, :]
        out_ref[begin:begin + half, :] = jnp.where(left, first, pltpu.roll(second, 64, 1))
        out_ref[begin + half:begin + half + 8, :] = jnp.broadcast_to(exponent, (8, 128))


def project(tri, start, x, pos, owners, cap):
    feature, width = start.shape
    return pl.pallas_call(
        functools.partial(project_kernel, cap),
        out_shape=(
            jax.ShapeDtypeStruct((owners * packed_rows(cap), 128), jnp.int32),
            jax.ShapeDtypeStruct((feature, 2 * width), jnp.bfloat16),
            jax.ShapeDtypeStruct((width, width), jnp.float32),
        ),
        in_specs=[vmem(), vmem(), pl.BlockSpec(memory_space=pl.ANY), smem()],
        out_specs=(vmem(), vmem(), vmem()),
        scratch_shapes=[
            pltpu.VMEM(x.shape, jnp.bfloat16),
            pltpu.SemaphoreType.DMA,
            pltpu.VMEM((feature, feature), jnp.bfloat16),
            pltpu.VMEM((feature, feature), jnp.bfloat16),
            pltpu.VMEM((2 * x.shape[0], 128), jnp.float32),
            pltpu.VMEM((x.shape[0], 128), jnp.int32),
            pltpu.VMEM((x.shape[0], 128), jnp.int32),
            pltpu.VMEM((owners * cap, 128), jnp.int32),
        ],
        compiler_params=limits(),
        cost_estimate=pl.CostEstimate(flops=10**10, bytes_accessed=2 * 10**7, transcendentals=0),
        name="project",
    )(tri, start, x, pos)


def factor_kernel(gram_ref, inverse_ref, pivot_ref, aug):
    size = gram_ref.shape[0]
    block = 32
    panel = 8
    aug[:, :size] = gram_ref[...]
    aug[:, size:] = (
        lax.broadcasted_iota(jnp.int32, (size, size), 0) == lax.broadcasted_iota(jnp.int32, (size, size), 1)
    ).astype(jnp.float32)
    row_at = lax.broadcasted_iota(jnp.int32, (block, 128), 0)
    lane_at = lax.broadcasted_iota(jnp.int32, (block, 128), 1)
    least = jnp.full((1, 128), 1e30, jnp.float32)
    for b in range(size // block):
        lo, hi = b * block, (b + 1) * block
        square = aug[lo:hi, lo:hi]
        unit = (row_at[:, :block] == lane_at[:, :block]).astype(jnp.float32)
        work = jnp.concatenate([square, unit, jnp.zeros((block, 128 - 2 * block), jnp.float32)], axis=1)
        for p in range(block // panel):
            cols = [
                jnp.broadcast_to(work[:, p * panel + j:p * panel + j + 1], (block, 128)) for j in range(panel)
            ]
            for j in range(panel):
                k = p * panel + j
                pivot = cols[j][k:k + 1, :]
                least = jnp.minimum(least, pivot)
                root = lax.rsqrt(pivot)
                column = jnp.where(row_at > k, cols[j] * root, 0.0)
                for jj in range(j + 1, panel):
                    kk = p * panel + jj
                    cols[jj] = cols[jj] - column * column[kk:kk + 1, :]
                row = work[k:k + 1, :] * root
                work = jnp.where(row_at == k, row, work - column * row)
        inverse = work[:, block:2 * block]
        rows = lax.dot_general(inverse, aug[lo:hi, :], (((1,), (0,)), ((), ())), precision=lax.Precision.HIGHEST,
                               preferred_element_type=jnp.float32)
        aug[lo:hi, :] = rows
        if hi < size:
            below = rows[:, hi:size].T
            aug[hi:, :] -= lax.dot_general(below, rows, (((1,), (0,)), ((), ())), precision=lax.Precision.HIGHEST,
                                           preferred_element_type=jnp.float32)
    whole = aug[:, size:].T
    top, bottom = halves(whole)
    inverse_ref[:, :size] = top
    inverse_ref[:, size:] = bottom
    pivot_ref[...] = least


def factor(gram):
    size = gram.shape[0]
    return pl.pallas_call(
        factor_kernel,
        out_shape=(
            jax.ShapeDtypeStruct((size, 2 * size), jnp.bfloat16),
            jax.ShapeDtypeStruct((1, 128), jnp.float32),
        ),
        in_specs=[vmem()],
        out_specs=(vmem(), vmem()),
        scratch_shapes=[pltpu.VMEM((size, 2 * size), jnp.float32)],
        compiler_params=limits(),
        cost_estimate=pl.CostEstimate(flops=10**9, bytes_accessed=10**7, transcendentals=0),
        name="factor",
    )(gram)


def offset_kernel(cap, c_ref, basis_ref, id_ref, out_ref, z_ref):
    project_rows(c_ref, basis_ref, z_ref)
    count = c_ref.shape[0]

    @pl.loop(0, id_ref.shape[0] // cap)
    def _(sender):
        @pl.loop(0, cap // 16)
        def _(k):
            for u in range(16):
                rank = k * 16 + u
                row = jnp.maximum(id_ref[sender * cap + rank], 0)
                slot = sender * (2 * cap) + rank
                out_ref[pl.ds(slot, 1), :] = z_ref[pl.ds(row, 1), :]
                out_ref[pl.ds(slot + cap, 1), :] = z_ref[pl.ds(row + count, 1), :]


def offsets_at(centroids, basis, ids, cap):
    return pl.pallas_call(
        functools.partial(offset_kernel, cap),
        out_shape=jax.ShapeDtypeStruct((2 * ids.shape[0], 128), jnp.float32),
        in_specs=[vmem(), vmem(), smem()],
        out_specs=vmem(),
        scratch_shapes=[pltpu.VMEM((2 * centroids.shape[0], 128), jnp.float32)],
        compiler_params=limits(),
        cost_estimate=pl.CostEstimate(flops=10**10, bytes_accessed=10**7, transcendentals=0),
        name="offsets",
    )(centroids, basis, ids)


def finish_kernel(senders, z_ref, off_ref, count_ref, inverse_ref, out_ref):
    width = out_ref.shape[1]
    cap = out_ref.shape[0] // senders
    rank = lax.broadcasted_iota(jnp.int32, (cap, width), 0)
    half = cap // 2
    left = lax.broadcasted_iota(jnp.int32, (half, 128), 1) < 64
    gaps = []
    for s in range(senders):
        begin = s * packed_rows(cap)
        word = z_ref[begin:begin + cap, :]
        tail = z_ref[begin + cap:begin + cap + half, :]
        unit = step_of(z_ref[begin + cap + half:begin + cap + half + 1, :])
        upper = tail >> 16
        under = (tail << 16) >> 16
        first = jnp.where(left, upper, pltpu.roll(under, 64, 1))
        second = jnp.where(left, pltpu.roll(upper, 64, 1), under)
        high = (jnp.concatenate([first, second], axis=0) << 8) | (word & 255)
        begin = 2 * s * cap
        low = (word >> 8).astype(jnp.float32) * unit - off_ref[begin:begin + cap, :]
        high = high.astype(jnp.float32) * unit - off_ref[begin + cap:begin + 2 * cap, :]
        gaps.append(jnp.concatenate([low, high], axis=1))
    hi, lo = halves(jnp.concatenate(gaps, axis=0))
    both = dot(hi, inverse_ref[...])
    code = (both[:, :width] + both[:, width:]) + dot(lo, inverse_ref[:, :width])
    for s in range(senders):
        filled = rank < count_ref[pl.program_id(0) * senders + s]
        at = slice(s * cap, (s + 1) * cap)
        out_ref[at, :] = jnp.where(filled, code[at, :], 0.0).astype(jnp.bfloat16)


def finish(z, off, filled, inverse):
    owners = filled.shape[0]
    slots = off.shape[0] // 2
    width = inverse.shape[0]
    senders = 4
    step = senders * (slots // owners)
    return pl.pallas_call(
        functools.partial(finish_kernel, senders),
        out_shape=jax.ShapeDtypeStruct((slots, width), jnp.bfloat16),
        grid=(slots // step,),
        in_specs=[
            pl.BlockSpec((z.shape[0] // owners * senders, 128), lambda s: (s, 0)),
            pl.BlockSpec((2 * step, 128), lambda s: (s, 0)),
            smem(),
            pl.BlockSpec((width, 2 * width), lambda s: (0, 0)),
        ],
        out_specs=pl.BlockSpec((step, width), lambda s: (s, 0)),
        compiler_params=limits(),
        cost_estimate=pl.CostEstimate(flops=2 * 10**9, bytes_accessed=13 * 10**6, transcendentals=0),
        name="finish",
    )(z, off, filled, inverse)


exact_mode = lax.Precision.HIGHEST
PIVOT_LEAST = 1.0 / 64.0


def orthonormal(product):
    gram_matrix = jnp.dot(product.T, product, precision=exact_mode, preferred_element_type=jnp.float32)
    lower = jnp.linalg.cholesky(gram_matrix)
    return jax.scipy.linalg.solve_triangular(lower, product.T, lower=True).T


def careful(tri, start, x, centroids, pos, ids):
    owners = lax.axis_size("dev")
    slots = ids.shape[0]
    grid = [[None] * 8 for _ in range(8)]
    for i in range(8):
        for j in range(i + 1):
            at = STARTS[(i, j)]
            grid[i][j] = tri[at:at + 128]
            grid[j][i] = tri[at:at + 128].T
    moment = jnp.block(grid)
    basis = start
    for sweep in range(2):
        product = jnp.dot(moment, basis, precision=exact_mode, preferred_element_type=jnp.float32)
        basis = orthonormal(product)
    width = start.shape[1]
    projected = jnp.dot(x, basis, precision=exact_mode, preferred_element_type=jnp.float32)
    sent = jnp.zeros((slots, width), jnp.float32).at[pos[0]].set(projected)
    sent = sent.reshape(owners, slots // owners, width)
    values = lax.all_to_all(sent, "dev", split_axis=0, concat_axis=0, tiled=True).reshape(slots, width)
    offsets = jnp.dot(centroids, basis, precision=exact_mode, preferred_element_type=jnp.float32)
    code = values - jnp.take(offsets, jnp.maximum(ids, 0), axis=0)
    return jnp.where(ids[:, None] >= 0, code, 0.0).astype(jnp.bfloat16)


def shards(corpus_rows, list_ids, source_ids, list_slot, centroids, start_basis):
    owners = lax.axis_size("dev")
    lists_dev = centroids.shape[0]
    slots = owners * CAP
    tri, pos, arrived, counts = front(corpus_rows, list_ids, source_ids, list_slot, owners, lists_dev, CAP)
    sent, basis, gram = project(tri, start_basis, corpus_rows, pos, owners, CAP)
    values = lax.all_to_all(
        sent.reshape(owners, packed_rows(CAP), 128), "dev", split_axis=0, concat_axis=0, tiled=True
    ).reshape(owners * packed_rows(CAP), 128)
    ids = arrived[:, :2].reshape(owners, 256)[:, :CAP]
    filled = jnp.sum((ids >= 0).astype(jnp.int32), axis=1)
    ids = ids.reshape(slots)
    row_sources = arrived[:, 2:].reshape(owners, 256)[:, :CAP].reshape(slots)
    inverse, pivots = factor(gram)
    off = offsets_at(centroids, basis, ids, CAP)
    row_codes = lax.cond(
        jnp.min(pivots) >= PIVOT_LEAST,
        lambda codes: codes,
        lambda codes: careful(tri, start_basis, corpus_rows, centroids, pos, ids),
        finish(values, off, filled, inverse),
    )
    return row_codes, row_sources, counts.reshape(lists_dev)


def solution(mesh):
    placed = (
        P(("group", "dev"), None),
        P(("group", "dev")),
        P(("group", "dev")),
        P(),
        P("dev", None),
        P(),
    )
    return jax.shard_map(
        shards,
        mesh=mesh,
        in_specs=placed,
        out_specs=(P(("group", "dev"), None), P(("group", "dev")), P("dev")),
        check_vma=False,
    )
```

profile of v0, /device:TPU:8, one launch (start us, length us, event | category | flops | bytes accessed | tf_op | source)
XLA Modules:
  0.0 141.3 jit_solution(12641615165907470184)
XLA Ops:
  0.6 0.0 copy-start.2
  0.6 50.7 %front.1 = (f32[4608,128]{1,0:T(8,128)}, s32[2,2048]{1,0:T(2,128)S(1)}, s32[32,4,128]{2,1,0:T(4,128)}, s32[16,128]{1,0:T(8,128)}) custom-call(bf16[2048,1024]{1,0:T(8,128)(2,1)} %x_hbm.3, s32[1,2048]{1,0:T(1,128)} %bitcast.193, s32[1,2048]{1,0:T(1,128)} %bitcast.194, s32[512,128]{1,0:T(8,128)} %bitcast.192), custom_call_target="tpu_custom_call" | custom-call | flops 10000000000 | bytes 100000000 | tf_op jit(solution)/shard_map/front/pallas_call | solution.py:315
  51.3 0.0 copy-start.8
  51.3 0.0 copy-done.2
  51.3 19.7 %project.1 = (s32[7936,128]{1,0:T(8,128)S(1)}, bf16[1024,512]{1,0:T(8,128)(2,1)S(1)}, f32[256,256]{1,0:T(8,128)S(1)}) custom-call(f32[4608,128]{1,0:T(8,128)} %get-tuple-element.39.tri_ref, f32[1024,256]{1,0:T(8,128)S(1)} %copy-done.2, bf16[2048,1024]{1,0:T(8,128)(2,1)} %x_hbm.3, s32[2,2048]{1,0:T(2,128)S(1)} %get-tuple-element.40.pos_ref), custom_call_target="tpu_custom_call" | custom-call | flops 10000000000 | bytes 20000000 | tf_op jit(solution)/shard_map/project/pallas_call | solution.py:445
  71.1 0.0 copy-done.8
  71.1 0.0 copy-start
  71.1 2.0 %copy-done = s32[7936,128]{1,0:T(8,128)} copy-done((s32[7936,128]{1,0:T(8,128)}, s32[7936,128]{1,0:T(8,128)S(1)}, u32[]{:S(2)}) %copy-start) | copy-done | bytes 4063256
  73.1 0.0 copy-start.6
  73.1 5.8 %all-to-all-start.1 = ((s32[32,248,128]{2,1,0:T(8,128)}), s32[32,248,128]{2,1,0:T(8,128)}, u32[]{:S(2)}, u32[]{:S(2)}) async-start(s32[32,248,128]{2,1,0:T(8,128)} %bitcast.180), calls=%async_computation.1 | async-start | bytes 8126464 | tf_op jit(solution)/shard_map/all_to_all | solution.py:655
  78.9 11.3 %factor.1 = (bf16[256,512]{1,0:T(8,128)(2,1)S(1)}, f32[1,128]{1,0:T(1,128)S(1)}) custom-call(f32[256,256]{1,0:T(8,128)S(1)} %get-tuple-element.41.gram_ref), custom_call_target="tpu_custom_call" | custom-call | flops 1000000000 | bytes 10000000 | tf_op jit(solution)/shard_map/factor/pallas_call | solution.py:518
  90.3 0.6 reduce_min.9
  91.5 0.0 copy-done.6
  91.6 0.1 convert_reduce_fusion
  91.7 0.1 reshape.103.id_ref
  91.8 0.7 reshape.107
  92.5 0.0 copy-start.9
  92.5 16.5 %offsets.1.off_ref = f32[10240,128]{1,0:T(8,128)} custom-call(bf16[2048,1024]{1,0:T(8,128)(2,1)} %c_ref.1, bf16[1024,512]{1,0:T(8,128)(2,1)S(1)} %get-tuple-element.45.basis_ref, s32[5120]{0:T(1024)S(1)} %reshape.103.id_ref), custom_call_target="tpu_custom_call" | custom-call | flops 10000000000 | bytes 10000000 | tf_op jit(solution)/shard_map/offsets/pallas_call | solution.py:550
  109.0 22.1 %all-to-all-done.1 = s32[32,248,128]{2,1,0:T(8,128)} async-done(((s32[32,248,128]{2,1,0:T(8,128)}), s32[32,248,128]{2,1,0:T(8,128)}, u32[]{:S(2)}, u32[]{:S(2)}) %all-to-all-start.1) | async-done | bytes 4063264 | tf_op jit(solution)/shard_map/all_to_all | solution.py:655
  131.1 0.0 copy-done.9
  131.1 8.9 %finish.1 = bf16[5120,256]{1,0:T(8,128)(2,1)} custom-call(s32[7936,128]{1,0:T(8,128)} %bitcast.58.z_ref, f32[10240,128]{1,0:T(8,128)} %offsets.1.off_ref, s32[32]{0:T(128)S(1)} %get-tuple-element.131.count_ref, bf16[256,512]{1,0:T(8,128)(2,1)S(1)} %get-tuple-element.46.inverse_ref), custom_call_target="tpu_custom_call" | custom-call | flops 2000000000 | bytes 13000000 | tf_op jit(solution)/shard_map/finish/pallas_call | solution.py:598
  140.0 0.0 copy-start.7
  140.0 0.7 copy-done.7
  140.7 0.6 copy.174
  (4 shorter events, 0.0 us)
Async XLA Ops:
  0.6 50.7 %copy-start.2 = (f32[1024,256]{1,0:T(8,128)S(1)}, f32[1024,256]{1,0:T(8,128)}, u32[]{:S(2)}) copy-start(f32[1024,256]{1,0:T(8,128)} %start_ref.1) | copy-start | bytes 3145732
  51.3 19.7 %copy-start.8 = (s32[2,2048]{1,0:T(2,128)}, s32[2,2048]{1,0:T(2,128)S(1)}, u32[]{:S(2)}) copy-start(s32[2,2048]{1,0:T(2,128)S(1)} %get-tuple-element.40.pos_ref) | copy-start | bytes 49156
  71.1 2.0 %copy-start = (s32[7936,128]{1,0:T(8,128)}, s32[7936,128]{1,0:T(8,128)S(1)}, u32[]{:S(2)}) copy-start(s32[7936,128]{1,0:T(8,128)S(1)} %get-tuple-element.44) | copy-start | bytes 12189700
  73.1 18.4 %copy-start.6 = (s32[32,4,128]{2,1,0:T(4,128)S(1)}, s32[32,4,128]{2,1,0:T(4,128)}, u32[]{:S(2)}) copy-start(s32[32,4,128]{2,1,0:T(4,128)} %get-tuple-element.43) | copy-start | bytes 196612
  73.1 58.0 %all-to-all-start.1 = ((s32[32,248,128]{2,1,0:T(8,128)}), s32[32,248,128]{2,1,0:T(8,128)}, u32[]{:S(2)}, u32[]{:S(2)}) async-start(s32[32,248,128]{2,1,0:T(8,128)} %bitcast.180), calls=%async_computation.1 | async-start | bytes 8126464 | tf_op jit(solution)/shard_map/all_to_all | solution.py:655
  92.5 38.6 %copy-start.9 = (s32[2,2048]{1,0:T(2,128)S(1)}, s32[2,2048]{1,0:T(2,128)}, u32[]{:S(2)}) copy-start(s32[2,2048]{1,0:T(2,128)} %copy-done.8) | copy-start | bytes 49156
  140.0 0.7 copy-start.7
where the time goes:
time: 142 us; the launch traced here: 141 us
  Pallas kernels  107 us (75%)
  waiting for transfers between devices  22.1 us (16%)
  starting transfers between devices  5.83 us (4%)
  local copies, waits for them, and re-layouts  4.14 us (3%)
    pallas_call x1, Pallas kernels, front(): pl.pallas_call(functools.partial(front_kernel, lists_dev, cap), out_shape...  50.7 us
    all_to_all x1, waiting for transfers between devices, shards(): lax.all_to_all(sent.reshape(owners, packed_rows(CAP), 128), 'dev', split_...  22.1 us
    pallas_call x1, Pallas kernels, project(): pl.pallas_call(functools.partial(project_kernel, cap), out_shape=(jax.Sha...  19.7 us
    pallas_call x1, Pallas kernels, offsets_at(): pl.pallas_call(functools.partial(offset_kernel, cap), out_shape=jax.Shape...  16.5 us
    pallas_call x1, Pallas kernels, factor(): pl.pallas_call(factor_kernel, out_shape=(jax.ShapeDtypeStruct((size, 2 *...  11.3 us
    pallas_call x1, Pallas kernels, finish(): pl.pallas_call(functools.partial(finish_kernel, senders), out_shape=jax.S...  8.91 us
    all_to_all x1, starting transfers between devices, shards(): lax.all_to_all(sent.reshape(owners, packed_rows(CAP), 128), 'dev', split_...  5.83 us
    unnamed x15, local copies, waits for them, and re-layouts  3.35 us
  transfers between devices with their start and end apart: 1, of which 1 were waited for; matrix products, arithmetic and copies ran while one was open for 1% of the time, Pallas kernels for 20%

commit v1 on v0

--- a/solution.py
+++ b/solution.py
@@ -593,7 +593,7 @@
     owners = filled.shape[0]
     slots = off.shape[0] // 2
     width = inverse.shape[0]
-    senders = 4
+    senders = 8
     step = senders * (slots // owners)
     return pl.pallas_call(
         functools.partial(finish_kernel, senders),

time: 142 us -> 140 us (0.986)
  Pallas kernels: 107 us -> 105 us
    pallas_call x1, Pallas kernels: 8.91 us -> 6.89 us  [finish(): pl.pallas_call(functools.partial(finish_kernel, senders), out_shape=jax.S...]
where the time goes in v1:
time: 140 us; the launch traced here: 139 us
  Pallas kernels  105 us (75%)
  waiting for transfers between devices  22.1 us (16%)
  starting transfers between devices  5.83 us (4%)
  local copies, waits for them, and re-layouts  4.14 us (3%)
    pallas_call x1, Pallas kernels, front(): pl.pallas_call(functools.partial(front_kernel, lists_dev, cap), out_shape...  50.7 us
    all_to_all x1, waiting for transfers between devices, shards(): lax.all_to_all(sent.reshape(owners, packed_rows(CAP), 128), 'dev', split_...  22.1 us
    pallas_call x1, Pallas kernels, project(): pl.pallas_call(functools.partial(project_kernel, cap), out_shape=(jax.Sha...  19.7 us
    pallas_call x1, Pallas kernels, offsets_at(): pl.pallas_call(functools.partial(offset_kernel, cap), out_shape=jax.Shape...  16.5 us
    pallas_call x1, Pallas kernels, factor(): pl.pallas_call(factor_kernel, out_shape=(jax.ShapeDtypeStruct((size, 2 *...  11.3 us
    pallas_call x1, Pallas kernels, finish(): pl.pallas_call(functools.partial(finish_kernel, senders), out_shape=jax.S...  6.89 us
    all_to_all x1, starting transfers between devices, shards(): lax.all_to_all(sent.reshape(owners, packed_rows(CAP), 128), 'dev', split_...  5.83 us
    unnamed x15, local copies, waits for them, and re-layouts  3.35 us
  transfers between devices with their start and end apart: 1, of which 1 were waited for; matrix products, arithmetic and copies ran while one was open for 1% of the time, Pallas kernels for 20%

profile of v1, /device:TPU:8, one launch (start us, length us, event | category | flops | bytes accessed | tf_op | source)
XLA Modules:
  0.0 139.3 jit_solution(11063019752570997412)
XLA Ops:
  0.6 0.0 copy-start.2
  0.6 50.7 %front.1 = (f32[4608,128]{1,0:T(8,128)}, s32[2,2048]{1,0:T(2,128)S(1)}, s32[32,4,128]{2,1,0:T(4,128)}, s32[16,128]{1,0:T(8,128)}) custom-call(bf16[2048,1024]{1,0:T(8,128)(2,1)} %x_hbm.3, s32[1,2048]{1,0:T(1,128)} %bitcast.193, s32[1,2048]{1,0:T(1,128)} %bitcast.194, s32[512,128]{1,0:T(8,128)} %bitcast.192), custom_call_target="tpu_custom_call" | custom-call | flops 10000000000 | bytes 100000000 | tf_op jit(solution)/shard_map/front/pallas_call | solution.py:315
  51.3 0.0 copy-start.8
  51.3 0.0 copy-done.2
  51.3 19.7 %project.1 = (s32[7936,128]{1,0:T(8,128)S(1)}, bf16[1024,512]{1,0:T(8,128)(2,1)S(1)}, f32[256,256]{1,0:T(8,128)S(1)}) custom-call(f32[4608,128]{1,0:T(8,128)} %get-tuple-element.39.tri_ref, f32[1024,256]{1,0:T(8,128)S(1)} %copy-done.2, bf16[2048,1024]{1,0:T(8,128)(2,1)} %x_hbm.3, s32[2,2048]{1,0:T(2,128)S(1)} %get-tuple-element.40.pos_ref), custom_call_target="tpu_custom_call" | custom-call | flops 10000000000 | bytes 20000000 | tf_op jit(solution)/shard_map/project/pallas_call | solution.py:445
  71.1 0.0 copy-done.8
  71.1 0.0 copy-start
  71.1 2.0 %copy-done = s32[7936,128]{1,0:T(8,128)} copy-done((s32[7936,128]{1,0:T(8,128)}, s32[7936,128]{1,0:T(8,128)S(1)}, u32[]{:S(2)}) %copy-start) | copy-done | bytes 4063256
  73.1 0.0 copy-start.6
  73.1 5.8 %all-to-all-start.1 = ((s32[32,248,128]{2,1,0:T(8,128)}), s32[32,248,128]{2,1,0:T(8,128)}, u32[]{:S(2)}, u32[]{:S(2)}) async-start(s32[32,248,128]{2,1,0:T(8,128)} %bitcast.180), calls=%async_computation.1 | async-start | bytes 8126464 | tf_op jit(solution)/shard_map/all_to_all | solution.py:655
  78.9 11.3 %factor.1 = (bf16[256,512]{1,0:T(8,128)(2,1)S(1)}, f32[1,128]{1,0:T(1,128)S(1)}) custom-call(f32[256,256]{1,0:T(8,128)S(1)} %get-tuple-element.41.gram_ref), custom_call_target="tpu_custom_call" | custom-call | flops 1000000000 | bytes 10000000 | tf_op jit(solution)/shard_map/factor/pallas_call | solution.py:518
  90.3 0.6 reduce_min.9
  91.5 0.0 copy-done.6
  91.6 0.1 convert_reduce_fusion
  91.7 0.1 reshape.103.id_ref
  91.8 0.7 reshape.107
  92.5 0.0 copy-start.9
  92.5 16.5 %offsets.1.off_ref = f32[10240,128]{1,0:T(8,128)} custom-call(bf16[2048,1024]{1,0:T(8,128)(2,1)} %c_ref.1, bf16[1024,512]{1,0:T(8,128)(2,1)S(1)} %get-tuple-element.45.basis_ref, s32[5120]{0:T(1024)S(1)} %reshape.103.id_ref), custom_call_target="tpu_custom_call" | custom-call | flops 10000000000 | bytes 10000000 | tf_op jit(solution)/shard_map/offsets/pallas_call | solution.py:550
  109.0 22.1 %all-to-all-done.1 = s32[32,248,128]{2,1,0:T(8,128)} async-done(((s32[32,248,128]{2,1,0:T(8,128)}), s32[32,248,128]{2,1,0:T(8,128)}, u32[]{:S(2)}, u32[]{:S(2)}) %all-to-all-start.1) | async-done | bytes 4063264 | tf_op jit(solution)/shard_map/all_to_all | solution.py:655
  131.1 0.0 copy-done.9
  131.1 6.9 %finish.1 = bf16[5120,256]{1,0:T(8,128)(2,1)} custom-call(s32[7936,128]{1,0:T(8,128)} %bitcast.58.z_ref, f32[10240,128]{1,0:T(8,128)} %offsets.1.off_ref, s32[32]{0:T(128)S(1)} %get-tuple-element.131.count_ref, bf16[256,512]{1,0:T(8,128)(2,1)S(1)} %get-tuple-element.46.inverse_ref), custom_call_target="tpu_custom_call" | custom-call | flops 2000000000 | bytes 13000000 | tf_op jit(solution)/shard_map/finish/pallas_call | solution.py:598
  138.0 0.0 copy-start.7
  138.0 0.7 copy-done.7
  138.7 0.6 copy.174
  (4 shorter events, 0.0 us)
Async XLA Ops:
  0.6 50.7 %copy-start.2 = (f32[1024,256]{1,0:T(8,128)S(1)}, f32[1024,256]{1,0:T(8,128)}, u32[]{:S(2)}) copy-start(f32[1024,256]{1,0:T(8,128)} %start_ref.1) | copy-start | bytes 3145732
  51.3 19.7 %copy-start.8 = (s32[2,2048]{1,0:T(2,128)}, s32[2,2048]{1,0:T(2,128)S(1)}, u32[]{:S(2)}) copy-start(s32[2,2048]{1,0:T(2,128)S(1)} %get-tuple-element.40.pos_ref) | copy-start | bytes 49156
  71.1 2.0 %copy-start = (s32[7936,128]{1,0:T(8,128)}, s32[7936,128]{1,0:T(8,128)S(1)}, u32[]{:S(2)}) copy-start(s32[7936,128]{1,0:T(8,128)S(1)} %get-tuple-element.44) | copy-start | bytes 12189700
  73.1 18.4 %copy-start.6 = (s32[32,4,128]{2,1,0:T(4,128)S(1)}, s32[32,4,128]{2,1,0:T(4,128)}, u32[]{:S(2)}) copy-start(s32[32,4,128]{2,1,0:T(4,128)} %get-tuple-element.43) | copy-start | bytes 196612
  73.1 58.0 %all-to-all-start.1 = ((s32[32,248,128]{2,1,0:T(8,128)}), s32[32,248,128]{2,1,0:T(8,128)}, u32[]{:S(2)}, u32[]{:S(2)}) async-start(s32[32,248,128]{2,1,0:T(8,128)} %bitcast.180), calls=%async_computation.1 | async-start | bytes 8126464 | tf_op jit(solution)/shard_map/all_to_all | solution.py:655
  92.5 38.6 %copy-start.9 = (s32[2,2048]{1,0:T(2,128)S(1)}, s32[2,2048]{1,0:T(2,128)}, u32[]{:S(2)}) copy-start(s32[2,2048]{1,0:T(2,128)} %copy-done.8) | copy-start | bytes 49156
  138.0 0.7 copy-start.7
